TPU v7x, 1024 devices: a whole 8x8x8 slice. The times are simulated.
1024 devices in a mesh: depth: 64 (over x, z), tile: 16 (over y, core).
Axes of the slice: x: 8, y: 8, z: 8, core: 2. Of those that a mesh axis runs over, the one named last changes fastest.
Arguments:
- features: bfloat16 [32, 256, 131072], P(None, 'depth', 'tile'), may hold values from -6 to 6
- ray_spans: int32 [2, 64, 131072], P(None, 'depth', 'tile'), may hold values from 0 to 4, as said below
- view_order: int32 [16], P('tile'), may hold values 0 or 1
- w_first: bfloat16 [128, 32], replicated, may hold values from -1 to 1
- b_first: float32 [128], replicated, may hold values from -3 to 3
- w_second: bfloat16 [128, 128], replicated, may hold values from -0.5 to 0.5
- b_second: float32 [128], replicated, may hold values from -3 to 3
- w_last: bfloat16 [4, 128], replicated, may hold values from -0.5 to 0.5
- b_last: float32 [4], replicated, may hold values from -3 to 3
Outputs:
- image: float32 [4, 131072], P(None, ('tile', 'depth'))
Inputs may be any that keep to these rules, and one draw needn't show every extreme that they name: A ray samples positions ray_spans[0] to ray_spans[1] - 1 of its slab. Within each block of 1024 pixels (aligned, in one slab) either every ray has ray_spans[0] < ray_spans[1], or every ray has both equal to 0.
All inputs are finite; a program needn't handle non-finite values. No bound on the sum of `view_order` on one device may be relied on, other than what follows from the above.
Results may differ from a plain program's by a relative error of at most 0.00039.
Values may be sent and summed in bfloat16 or wider, within the bound.
A program may use at most 32 MiB of HBM per device.

v0:
```python
import jax
import jax.numpy as jnp
from jax import lax
from jax.sharding import PartitionSpec as P

BRICK_PIX = 1024


def partner(value, axis, bit):
    mask = 2**bit
    pairs = [(source, source ^ mask) for source in range(lax.axis_size(axis))]
    return lax.ppermute(value, axis, pairs)


def stack_over(layers, flipped):
    layers = jnp.where(flipped == 1, layers[::-1], layers)
    remain = 1.0 - layers[:, 3]
    through = jnp.concatenate([jnp.ones_like(remain[:1]), jnp.cumprod(remain, axis=0)[:-1]], axis=0)
    return jnp.sum(through[:, None] * layers, axis=0)


def decode(weights, voxels, entries, leaving, flipped, spacing):
    w_first, b_first, w_second, b_second, w_last, b_last = weights
    channels, samples, columns = voxels.shape
    stacked = voxels.reshape(channels, samples * columns)
    first = jax.nn.relu(
        jnp.dot(w_first, stacked, preferred_element_type=jnp.float32) + b_first[:, None]
    ).astype(jnp.bfloat16)
    second = jax.nn.relu(
        jnp.dot(w_second, first, preferred_element_type=jnp.float32) + b_second[:, None]
    ).astype(jnp.bfloat16)
    output = (
        jnp.dot(w_last, second, preferred_element_type=jnp.float32) + b_last[:, None]
    ).reshape(4, samples, columns)
    places = jnp.arange(samples, dtype=jnp.int32)[:, None]
    inside = (places >= entries[None, :]) & (places < leaving[None, :])
    opacity = jnp.where(inside, 1.0 - jnp.exp(-jax.nn.softplus(output[0]) * spacing), 0.0)
    shading = jax.nn.sigmoid(output[1:4])
    layers = jnp.concatenate([opacity[None] * shading, opacity[None]], axis=0)
    return stack_over(jnp.transpose(layers, (1, 0, 2)), flipped)


def guarded(wanted, weights, voxels, entries, leaving, flipped, spacing):
    return lax.cond(
        wanted,
        lambda: decode(weights, voxels, entries, leaving, flipped, spacing),
        lambda: jnp.zeros((4, entries.shape[0]), jnp.float32),
    )


def per_device(
    features, ray_spans, view_order, w_first, b_first, w_second, b_second, w_last, b_last
):
    weights = (w_first, b_first, w_second, b_second, w_last, b_last)
    channels, samples, pixels = features.shape
    slabs = lax.axis_size("depth")
    spacing = 6.0 / (samples * slabs)
    flipped = view_order[0]
    bricks = pixels // BRICK_PIX
    volume = features.reshape(channels, samples, bricks, BRICK_PIX)
    bounds = ray_spans.reshape(2, bricks, BRICK_PIX)
    occupied = (jnp.sum(bounds[1] - bounds[0], axis=1) > 0).astype(jnp.int32)
    moved = jnp.zeros((bricks,), dtype=jnp.bool_)
    results = jnp.stack(
        [
            guarded(
                (occupied[item] > 0) & jnp.logical_not(moved[item]),
                weights,
                volume[:, :, item],
                bounds[0, item],
                bounds[1, item],
                flipped,
                spacing,
            )
            for item in range(bricks)
        ]
    )
    partial_value = jnp.transpose(results, (1, 0, 2)).reshape(4, pixels)
    shares = pixels // slabs
    depth_index = lax.axis_index("depth")
    current = partial_value.reshape(4, slabs, shares)
    for bit in range(slabs.bit_length() - 1):
        paired = current.reshape(4, current.shape[1] // 2, 2, shares)
        upper_half = depth_index // 2**bit % 2
        retained = jnp.where(upper_half == 0, paired[:, :, 0], paired[:, :, 1])
        handed = jnp.where(upper_half == 0, paired[:, :, 1], paired[:, :, 0])
        received = partner(handed, "depth", bit)
        mine_first = (upper_half == 0) == (flipped == 0)
        nearer = jnp.where(mine_first, retained, received)
        farther = jnp.where(mine_first, received, retained)
        current = nearer + (1.0 - nearer[3:4]) * farther
    return current.reshape(4, shares)


def solution(mesh):
    return jax.shard_map(
        per_device,
        mesh=mesh,
        in_specs=(
            P(None, "depth", "tile"),
            P(None, "depth", "tile"),
            P("tile"),
            P(),
            P(),
            P(),
            P(),
            P(),
            P(),
        ),
        out_specs=P(None, ("tile", "depth")),
        check_vma=False,
    )
```

profile of v0, /device:TPU:2, one launch (start us, length us, event | category | flops | bytes accessed | tf_op | source)
XLA Modules:
  0.0 108.0 jit_solution(4097556357601636998)
XLA Ops:
  0.0 0.9 subtract_reduce_fusion
  0.9 1.0 reduce.17
  7.8 4.5 %reshape.1495 = bf16[32,4,8,1024]{3,2,1,0:T(8,128)(2,1)} reshape(bf16[32,4,8192]{2,1,0:T(4,128)(2,1)} %param.25) | data formatting | bytes 4194304 | tf_op jit(solution)/shard_map/reshape | solution.py:60
  12.3 1.9 %copy.101 = bf16[32,4,8,1024]{3,2,0,1:T(8,128)(2,1)S(1)} copy(bf16[32,4,8,1024]{3,2,1,0:T(8,128)(2,1)} %reshape.1495) | data formatting | bytes 4194304 | tf_op jit(solution)/shard_map/reshape | solution.py:60
  14.2 4.6 %conditional.8 = (f32[1,4,1024]{2,1,0:T(4,128)S(1)}) conditional(s32[]{:T(128)} %bitcast.49, () %tuple.69, (s32[]{:T(128)}, s32[2,8,1024]{2,1,0:T(8,128)S(1)}, bf16[32,4,8,1024]{3,2,0,1:T(8,128)(2,1)S(1)}, bf16[128,32]{0,1:T(8,128)(2,1)S(1)}, f32[128]{0:T(128)S(1)}, /*index=5*/bf16[128,128]{1,0:T(8,128)(2,1)S(1)}, f32[128]{0:T(128)S(1)}, ...), branch_computations={%region_1.0_spmd, %region_2.5_spmd} | conditional | flops 175378432 | bytes 8886314 | solution.py:44
  14.9 1.6 %copy.52 = bf16[32,4,8,1024]{3,1,0,2:T(4,128)(2,1)S(1)} copy(bf16[32,4,8,1024]{3,2,0,1:T(8,128)(2,1)S(1)} %get-tuple-element.431) | data formatting | bytes 4194304 | tf_op jit(solution)/shard_map
  18.8 4.6 %conditional.15 = (f32[1,4,1024]{2,1,0:T(4,128)S(1)}) conditional(s32[]{:T(128)} %bitcast.56, () %tuple.77, (s32[]{:T(128)}, s32[2,8,1024]{2,1,0:T(8,128)S(1)}, bf16[32,4,8,1024]{3,2,0,1:T(8,128)(2,1)S(1)}, bf16[128,32]{0,1:T(8,128)(2,1)S(1)}, f32[128]{0:T(128)S(1)}, /*index=5*/bf16[128,128]{1,0:T(8,128)(2,1)S(1)}, f32[128]{0:T(128)S(1)}, ...), branch_computations={%region_29.30_spmd, %region_30.33_spmd} | conditional | flops 175378432 | bytes 8886314 | solution.py:44
  19.5 1.6 %copy.66 = bf16[32,4,8,1024]{3,1,0,2:T(4,128)(2,1)S(1)} copy(bf16[32,4,8,1024]{3,2,0,1:T(8,128)(2,1)S(1)} %get-tuple-element.494) | data formatting | bytes 4194304 | tf_op jit(solution)/shard_map
  23.5 4.6 %conditional.14 = (f32[1,4,1024]{2,1,0:T(4,128)S(1)}) conditional(s32[]{:T(128)} %bitcast.55, () %tuple.76, (s32[]{:T(128)}, s32[2,8,1024]{2,1,0:T(8,128)S(1)}, bf16[32,4,8,1024]{3,2,0,1:T(8,128)(2,1)S(1)}, bf16[128,32]{0,1:T(8,128)(2,1)S(1)}, f32[128]{0:T(128)S(1)}, /*index=5*/bf16[128,128]{1,0:T(8,128)(2,1)S(1)}, f32[128]{0:T(128)S(1)}, ...), branch_computations={%region_25.26_spmd, %region_26.29_spmd} | conditional | flops 175378432 | bytes 8886314 | solution.py:44
  24.1 1.6 %copy.64 = bf16[32,4,8,1024]{3,1,0,2:T(4,128)(2,1)S(1)} copy(bf16[32,4,8,1024]{3,2,0,1:T(8,128)(2,1)S(1)} %get-tuple-element.485) | data formatting | bytes 4194304 | tf_op jit(solution)/shard_map
  28.1 4.8 %conditional.13 = (f32[1,4,1024]{2,1,0:T(4,128)S(1)}) conditional(s32[]{:T(128)} %bitcast.54, () %tuple.75, (s32[]{:T(128)}, s32[2,8,1024]{2,1,0:T(8,128)S(1)}, bf16[32,4,8,1024]{3,2,0,1:T(8,128)(2,1)S(1)}, bf16[128,32]{0,1:T(8,128)(2,1)S(1)}, f32[128]{0:T(128)S(1)}, /*index=5*/bf16[128,128]{1,0:T(8,128)(2,1)S(1)}, f32[128]{0:T(128)S(1)}, ...), branch_computations={%region_21.22_spmd, %region_22.25_spmd} | conditional | flops 175378432 | bytes 8886314 | solution.py:44
  28.9 1.6 %copy.62 = bf16[32,4,8,1024]{3,1,0,2:T(4,128)(2,1)S(1)} copy(bf16[32,4,8,1024]{3,2,0,1:T(8,128)(2,1)S(1)} %get-tuple-element.476) | data formatting | bytes 4194304 | tf_op jit(solution)/shard_map
  32.9 4.6 %conditional.12 = (f32[1,4,1024]{2,1,0:T(4,128)S(1)}) conditional(s32[]{:T(128)} %bitcast.53, () %tuple.74, (s32[]{:T(128)}, s32[2,8,1024]{2,1,0:T(8,128)S(1)}, bf16[32,4,8,1024]{3,2,0,1:T(8,128)(2,1)S(1)}, bf16[128,32]{0,1:T(8,128)(2,1)S(1)}, f32[128]{0:T(128)S(1)}, /*index=5*/bf16[128,128]{1,0:T(8,128)(2,1)S(1)}, f32[128]{0:T(128)S(1)}, ...), branch_computations={%region_17.18_spmd, %region_18.21_spmd} | conditional | flops 175378432 | bytes 8886314 | solution.py:44
  33.6 1.6 %copy.60 = bf16[32,4,8,1024]{3,1,0,2:T(4,128)(2,1)S(1)} copy(bf16[32,4,8,1024]{3,2,0,1:T(8,128)(2,1)S(1)} %get-tuple-element.467) | data formatting | bytes 4194304 | tf_op jit(solution)/shard_map
  37.5 4.6 %conditional.11 = (f32[1,4,1024]{2,1,0:T(4,128)S(1)}) conditional(s32[]{:T(128)} %bitcast.52, () %tuple.73, (s32[]{:T(128)}, s32[2,8,1024]{2,1,0:T(8,128)S(1)}, bf16[32,4,8,1024]{3,2,0,1:T(8,128)(2,1)S(1)}, bf16[128,32]{0,1:T(8,128)(2,1)S(1)}, f32[128]{0:T(128)S(1)}, /*index=5*/bf16[128,128]{1,0:T(8,128)(2,1)S(1)}, f32[128]{0:T(128)S(1)}, ...), branch_computations={%region_13.14_spmd, %region_14.17_spmd} | conditional | flops 175378432 | bytes 8886314 | solution.py:44
  38.2 1.6 %copy.58 = bf16[32,4,8,1024]{3,1,0,2:T(4,128)(2,1)S(1)} copy(bf16[32,4,8,1024]{3,2,0,1:T(8,128)(2,1)S(1)} %get-tuple-element.458) | data formatting | bytes 4194304 | tf_op jit(solution)/shard_map
  42.1 4.9 %conditional.10 = (f32[1,4,1024]{2,1,0:T(4,128)S(1)}) conditional(s32[]{:T(128)} %bitcast.51, () %tuple.72, (s32[]{:T(128)}, s32[2,8,1024]{2,1,0:T(8,128)S(1)}, bf16[32,4,8,1024]{3,2,0,1:T(8,128)(2,1)S(1)}, bf16[128,32]{0,1:T(8,128)(2,1)S(1)}, f32[128]{0:T(128)S(1)}, /*index=5*/bf16[128,128]{1,0:T(8,128)(2,1)S(1)}, f32[128]{0:T(128)S(1)}, ...), branch_computations={%region_9.10_spmd, %region_10.13_spmd} | conditional | flops 175378432 | bytes 8890650 | solution.py:44
  43.1 1.6 %copy.56 = bf16[32,4,8,1024]{3,1,0,2:T(4,128)(2,1)S(1)} copy(bf16[32,4,8,1024]{3,2,0,1:T(8,128)(2,1)S(1)} %get-tuple-element.449) | data formatting | bytes 4194304 | tf_op jit(solution)/shard_map
  47.0 4.7 %conditional.9 = (f32[1,4,1024]{2,1,0:T(4,128)S(1)}) conditional(s32[]{:T(128)} %bitcast.50, () %tuple.71, (s32[]{:T(128)}, s32[2,8,1024]{2,1,0:T(8,128)S(1)}, bf16[32,4,8,1024]{3,2,0,1:T(8,128)(2,1)S(1)}, bf16[128,32]{0,1:T(8,128)(2,1)S(1)}, f32[128]{0:T(128)S(1)}, /*index=5*/bf16[128,128]{1,0:T(8,128)(2,1)S(1)}, f32[128]{0:T(128)}, ...), branch_computations={%region_5.6_spmd, %region_6.9_spmd} | conditional | flops 175378432 | bytes 8888482 | solution.py:44
  47.7 1.6 %copy.54 = bf16[32,4,8,1024]{3,1,0,2:T(4,128)(2,1)S(1)} copy(bf16[32,4,8,1024]{3,2,0,1:T(8,128)(2,1)S(1)} %get-tuple-element.440) | data formatting | bytes 4194304 | tf_op jit(solution)/shard_map
  52.1 1.9 %collective-permute-start = (f32[4,32,128]{2,1,0:T(8,128)S(1)}, f32[4,32,128]{2,1,0:T(8,128)S(1)}, u32[]{:S(2)}, u32[]{:S(2)}) collective-permute-start(f32[4,32,128]{2,1,0:T(8,128)S(1)} %bitcast.343), channel_id=1, source_target_pairs={{0,16},{16,0},{32,48},{48,32},{64,80},{80,64},{96,112},{112,96},{1... | collective-permute-start | bytes 196616 | tf_op jit(solution)/shard_map/ppermute | solution.py:12
  54.7 3.9 %collective-permute-done = f32[4,32,128]{2,1,0:T(8,128)S(1)} collective-permute-done((f32[4,32,128]{2,1,0:T(8,128)S(1)}, f32[4,32,128]{2,1,0:T(8,128)S(1)}, u32[]{:S(2)}, u32[]{:S(2)}) %collective-permute-start) | collective-permute-done | bytes 65568 | tf_op jit(solution)/shard_map/ppermute | solution.py:12
  58.8 1.9 %collective-permute-start.1 = (f32[4,16,128]{2,1,0:T(8,128)S(1)}, f32[4,16,128]{2,1,0:T(8,128)S(1)}, u32[]{:S(2)}, u32[]{:S(2)}) collective-permute-start(f32[4,16,128]{2,1,0:T(8,128)S(1)} %bitcast.405), channel_id=1, source_target_pairs={{0,32},{16,48},{32,0},{48,16},{64,96},{80,112},{96,64},{112,80},{1... | collective-permute-start | bytes 98312 | tf_op jit(solution)/shard_map/ppermute | solution.py:12
  60.7 4.7 %collective-permute-done.1 = f32[4,16,128]{2,1,0:T(8,128)S(1)} collective-permute-done((f32[4,16,128]{2,1,0:T(8,128)S(1)}, f32[4,16,128]{2,1,0:T(8,128)S(1)}, u32[]{:S(2)}, u32[]{:S(2)}) %collective-permute-start.1) | collective-permute-done | bytes 32800 | tf_op jit(solution)/shard_map/ppermute | solution.py:12
  65.6 5.3 %collective-permute-start.2 = (f32[4,8,128]{2,1,0:T(8,128)S(1)}, f32[4,8,128]{2,1,0:T(8,128)S(1)}, u32[]{:S(2)}, u32[]{:S(2)}) collective-permute-start(f32[4,8,128]{2,1,0:T(8,128)S(1)} %bitcast.411), channel_id=1, source_target_pairs={{0,64},{16,80},{32,96},{48,112},{64,0},{80,16},{96,32},{112,48},{1... | collective-permute-start | bytes 49160 | tf_op jit(solution)/shard_map/ppermute | solution.py:12
  71.0 4.1 %collective-permute-done.2 = f32[4,8,128]{2,1,0:T(8,128)S(1)} collective-permute-done((f32[4,8,128]{2,1,0:T(8,128)S(1)}, f32[4,8,128]{2,1,0:T(8,128)S(1)}, u32[]{:S(2)}, u32[]{:S(2)}) %collective-permute-start.2) | collective-permute-done | bytes 16416 | tf_op jit(solution)/shard_map/ppermute | solution.py:12
  75.2 14.7 %collective-permute-start.3 = (f32[4,4,128]{2,1,0:T(4,128)S(1)}, f32[4,4,128]{2,1,0:T(4,128)S(1)}, u32[]{:S(2)}, u32[]{:S(2)}) collective-permute-start(f32[4,4,128]{2,1,0:T(4,128)S(1)} %bitcast.412), channel_id=1, source_target_pairs={{0,128},{16,144},{32,160},{48,176},{64,192},{80,208},{96,224},{112... | collective-permute-start | bytes 24584 | tf_op jit(solution)/shard_map/ppermute | solution.py:12
  89.9 1.6 %collective-permute-done.3 = f32[4,4,128]{2,1,0:T(4,128)S(1)} collective-permute-done((f32[4,4,128]{2,1,0:T(4,128)S(1)}, f32[4,4,128]{2,1,0:T(4,128)S(1)}, u32[]{:S(2)}, u32[]{:S(2)}) %collective-permute-start.3) | collective-permute-done | bytes 8224 | tf_op jit(solution)/shard_map/ppermute | solution.py:12
  91.6 1.9 %collective-permute-start.4 = (f32[4,2,128]{2,1,0:T(2,128)S(1)}, f32[4,2,128]{2,1,0:T(2,128)S(1)}, u32[]{:S(2)}, u32[]{:S(2)}) collective-permute-start(f32[4,2,128]{2,1,0:T(2,128)S(1)} %bitcast.413), channel_id=1, source_target_pairs={{0,256},{16,272},{32,288},{48,304},{64,320},{80,336},{96,352},{112... | collective-permute-start | bytes 12296 | tf_op jit(solution)/shard_map/ppermute | solution.py:12
  93.5 4.4 %collective-permute-done.4 = f32[4,2,128]{2,1,0:T(2,128)S(1)} collective-permute-done((f32[4,2,128]{2,1,0:T(2,128)S(1)}, f32[4,2,128]{2,1,0:T(2,128)S(1)}, u32[]{:S(2)}, u32[]{:S(2)}) %collective-permute-start.4) | collective-permute-done | bytes 4128 | tf_op jit(solution)/shard_map/ppermute | solution.py:12
  98.0 3.7 %collective-permute-start.5 = (f32[4,1,128]{2,0,1:T(4,128)S(1)}, f32[4,1,128]{2,0,1:T(4,128)S(1)}, u32[]{:S(2)}, u32[]{:S(2)}) collective-permute-start(f32[4,1,128]{2,0,1:T(4,128)S(1)} %bitcast.414), channel_id=1, source_target_pairs={{0,512},{16,528},{32,544},{48,560},{64,576},{80,592},{96,608},{112... | collective-permute-start | bytes 6152 | tf_op jit(solution)/shard_map/ppermute | solution.py:12
  101.7 5.7 %collective-permute-done.5 = f32[4,1,128]{2,0,1:T(4,128)S(1)} collective-permute-done((f32[4,1,128]{2,0,1:T(4,128)S(1)}, f32[4,1,128]{2,0,1:T(4,128)S(1)}, u32[]{:S(2)}, u32[]{:S(2)}) %collective-permute-start.5) | collective-permute-done | bytes 2080 | tf_op jit(solution)/shard_map/ppermute | solution.py:12
  (223 shorter events, 19.8 us)
Async XLA Ops:
  12.2 1.9 %copy-start = (bf16[128,32]{0,1:T(8,128)(2,1)S(1)}, bf16[128,32]{0,1:T(8,128)(2,1)}, u32[]{:S(2)}) copy-start(bf16[128,32]{0,1:T(8,128)(2,1)} %param.28) | copy-start | bytes 24580
  12.3 1.9 %copy-start.1 = (f32[128]{0:T(128)S(1)}, f32[128]{0:T(128)}, u32[]{:S(2)}) copy-start(f32[128]{0:T(128)} %param.29) | copy-start | bytes 1540
  12.3 1.9 %copy-start.2 = (bf16[128,128]{1,0:T(8,128)(2,1)S(1)}, bf16[128,128]{1,0:T(8,128)(2,1)}, u32[]{:S(2)}) copy-start(bf16[128,128]{1,0:T(8,128)(2,1)} %param.30) | copy-start | bytes 98308
  12.3 1.9 %copy-start.3 = (bf16[4,128]{1,0:T(4,128)(2,1)S(1)}, bf16[4,128]{1,0:T(4,128)(2,1)}, u32[]{:S(2)}) copy-start(bf16[4,128]{1,0:T(4,128)(2,1)} %param.32) | copy-start | bytes 3076
  12.3 1.9 %copy-start.4 = (f32[128]{0:T(128)S(1)}, f32[128]{0:T(128)}, u32[]{:S(2)}) copy-start(f32[128]{0:T(128)} %param.31) | copy-start | bytes 1540
  12.3 1.9 %copy-start.8 = (f32[4]{0:T(128)S(1)}, f32[4]{0:T(128)}, u32[]{:S(2)}) copy-start(f32[4]{0:T(128)} %param.33) | copy-start | bytes 52
  42.4 0.7 copy-start.5
  42.4 0.7 copy-start.9
  44.7 0.7 copy-start.6
  44.7 0.7 copy-start.10
  49.3 0.7 copy-start.7
  49.4 0.7 copy-start.11
  52.1 6.5 %collective-permute-start = (f32[4,32,128]{2,1,0:T(8,128)S(1)}, f32[4,32,128]{2,1,0:T(8,128)S(1)}, u32[]{:S(2)}, u32[]{:S(2)}) collective-permute-start(f32[4,32,128]{2,1,0:T(8,128)S(1)} %bitcast.343), channel_id=1, source_target_pairs={{0,16},{16,0},{32,48},{48,32},{64,80},{80,64},{96,112},{112,96},{1... | collective-permute-start | bytes 196616 | tf_op jit(solution)/shard_map/ppermute | solution.py:12
  58.8 6.7 %collective-permute-start.1 = (f32[4,16,128]{2,1,0:T(8,128)S(1)}, f32[4,16,128]{2,1,0:T(8,128)S(1)}, u32[]{:S(2)}, u32[]{:S(2)}) collective-permute-start(f32[4,16,128]{2,1,0:T(8,128)S(1)} %bitcast.405), channel_id=1, source_target_pairs={{0,32},{16,48},{32,0},{48,16},{64,96},{80,112},{96,64},{112,80},{1... | collective-permute-start | bytes 98312 | tf_op jit(solution)/shard_map/ppermute | solution.py:12
  65.6 9.5 %collective-permute-start.2 = (f32[4,8,128]{2,1,0:T(8,128)S(1)}, f32[4,8,128]{2,1,0:T(8,128)S(1)}, u32[]{:S(2)}, u32[]{:S(2)}) collective-permute-start(f32[4,8,128]{2,1,0:T(8,128)S(1)} %bitcast.411), channel_id=1, source_target_pairs={{0,64},{16,80},{32,96},{48,112},{64,0},{80,16},{96,32},{112,48},{1... | collective-permute-start | bytes 49160 | tf_op jit(solution)/shard_map/ppermute | solution.py:12
  75.2 16.4 %collective-permute-start.3 = (f32[4,4,128]{2,1,0:T(4,128)S(1)}, f32[4,4,128]{2,1,0:T(4,128)S(1)}, u32[]{:S(2)}, u32[]{:S(2)}) collective-permute-start(f32[4,4,128]{2,1,0:T(4,128)S(1)} %bitcast.412), channel_id=1, source_target_pairs={{0,128},{16,144},{32,160},{48,176},{64,192},{80,208},{96,224},{112... | collective-permute-start | bytes 24584 | tf_op jit(solution)/shard_map/ppermute | solution.py:12
  91.6 6.4 %collective-permute-start.4 = (f32[4,2,128]{2,1,0:T(2,128)S(1)}, f32[4,2,128]{2,1,0:T(2,128)S(1)}, u32[]{:S(2)}, u32[]{:S(2)}) collective-permute-start(f32[4,2,128]{2,1,0:T(2,128)S(1)} %bitcast.413), channel_id=1, source_target_pairs={{0,256},{16,272},{32,288},{48,304},{64,320},{80,336},{96,352},{112... | collective-permute-start | bytes 12296 | tf_op jit(solution)/shard_map/ppermute | solution.py:12
  98.0 9.4 %collective-permute-start.5 = (f32[4,1,128]{2,0,1:T(4,128)S(1)}, f32[4,1,128]{2,0,1:T(4,128)S(1)}, u32[]{:S(2)}, u32[]{:S(2)}) collective-permute-start(f32[4,1,128]{2,0,1:T(4,128)S(1)} %bitcast.414), channel_id=1, source_target_pairs={{0,512},{16,528},{32,544},{48,560},{64,576},{80,592},{96,608},{112... | collective-permute-start | bytes 6152 | tf_op jit(solution)/shard_map/ppermute | solution.py:12
where the time goes:
time: 109 us; the launch traced here: 108 us
  starting transfers between devices  29.5 us (27%)
  local copies, waits for them, and re-layouts  25.3 us (23%)
  waiting for transfers between devices  24.5 us (22%)
  matrix products  10.4 us (10%)
  loops' own time  6.82 us (6%)
  between operations  6.17 us (6%)
  other arithmetic  5.25 us (5%)
    ppermute x6, starting transfers between devices, partner(): return lax.ppermute(value, axis, pairs)  29.5 us
    ppermute x6, waiting for transfers between devices, partner(): return lax.ppermute(value, axis, pairs)  24.5 us
    another operation x8, local copies, waits for them, and re-layouts  13 us
    another operation x8, loops' own time, guarded(): lax.cond(wanted, lambda: decode(weights, voxels, entries, leaving, flippe...  6.82 us
    dot_general x8, matrix products, decode(): jnp.dot(w_last, second, preferred_element_type=jnp.float32)  6.72 us
    reshape x2, local copies, waits for them, and re-layouts, per_device(): volume = features.reshape(channels, samples, bricks, BRICK_PIX)  6.33 us
    dot_general x8, matrix products, decode(): jnp.dot(w_first, stacked, preferred_element_type=jnp.float32)  3.67 us
    rev x8, local copies, waits for them, and re-layouts, stack_over(): layers = jnp.where(flipped == 1, layers[::-1], layers)  2.28 us
  transfers between devices with their start and end apart: 6, of which 6 were waited for; matrix products, arithmetic and copies ran while one was open for 0% of the time, Pallas kernels for 0%

commit v1 on v0

v1 whole, which is shorter than its diff:
```python
import functools

import jax
import jax.numpy as jnp
from jax import lax
from jax.experimental import pallas as pl
from jax.experimental.pallas import tpu as pltpu
from jax.sharding import PartitionSpec as P

BF = jnp.bfloat16
F = jnp.float32
BRICK = 1024
CH = 32
NCH = 256 // CH
UNITS = ((0, 0), (0, 1), (1, 0), (1, 1))
MESH = pl.DeviceIdType.MESH


def over(near, far):
    through = 1.0 - near[3]
    return [a + through * b for a, b in zip(near, far)]


def ordered(flip, first, second):
    near = [jnp.where(flip, b, a) for a, b in zip(first, second)]
    far = [jnp.where(flip, a, b) for a, b in zip(first, second)]
    return over(near, far)


def stack_samples(z_ref, spans, zrow, row, flip, b_last, spacing):
    entry = spans[0, pl.ds(row, 8), :]
    leave = spans[1, pl.ds(row, 8), :]
    remain, opacity = [], []
    for s in range(4):
        density = z_ref[pl.ds(zrow + 4 * s, 8, stride=16), :] + b_last[0]
        soft = jnp.maximum(density, 0.0) + jnp.log1p(jnp.exp(-jnp.abs(density)))
        kept = jnp.exp(soft * (-spacing))
        kept = jnp.where((entry <= s) & (leave > s), kept, 1.0)
        remain.append(kept)
        opacity.append(1.0 - kept)
    p01 = remain[0] * remain[1]
    p012 = p01 * remain[2]
    q32 = remain[3] * remain[2]
    q321 = q32 * remain[1]
    through = [
        jnp.where(flip, q321, 1.0),
        jnp.where(flip, q32, remain[0]),
        jnp.where(flip, remain[3], p01),
        jnp.where(flip, 1.0, p012),
    ]
    weight = [t * o for t, o in zip(through, opacity)]
    layers = []
    for ch in range(3):
        total = None
        for s in range(4):
            color = z_ref[pl.ds(zrow + 4 * s + 1 + ch, 8, stride=16), :] + b_last[1 + ch]
            term = weight[s] * (0.5 * jnp.tanh(0.5 * color) + 0.5)
            total = term if total is None else total + term
        layers.append(total)
    layers.append((weight[0] + weight[1]) + (weight[2] + weight[3]))
    return layers


def kernel(*refs, slabs):
    accs = []
    for m in range(2):
        accs += [pltpu.ACC(m)((CH, 256), F)] * (2 * NCH)
        accs += [pltpu.ACC(m)((16, 256), F)] * 2 + [pltpu.ACC(m)((128, 256), F)]
    pl.run_scoped(lambda *accs: body(*refs, accs=accs, slabs=slabs), *accs)


def body(
    x_hbm, spans, order, w1t, w2, w3, b1, b2, bl_ref, out,
    xbuf, xs, w1p, w2p, w3p, bias, z_ref, h1s, h2s, sent, taken, sem, send_sem, recv_sem,
    *, accs, slabs,
):
    n = 2 * NCH + 3
    acc1 = [accs[m * n : m * n + NCH] for m in range(2)]
    acc2 = [accs[m * n + NCH : m * n + 2 * NCH] for m in range(2)]
    acc3 = [accs[m * n + 2 * NCH : m * n + 2 * NCH + 2] for m in range(2)]
    accw = [accs[m * n + 2 * NCH + 2] for m in range(2)]
    bricks = 8
    me = lax.axis_index("depth")
    low = lax.rem(me, 8)
    high = lax.div(me, 8)
    spacing = 6.0 / (4 * slabs)

    def place(k):
        return lax.rem(high + 1 + k, 8)

    def xcopy(k):
        start = pl.multiple_of(place(k) * BRICK, BRICK)
        return pltpu.make_async_copy(x_hbm.at[:, :, pl.ds(start, BRICK)], xbuf.at[k], sem.at[k])

    for k in range(bricks):
        xcopy(k).start()

    barrier = pltpu.get_barrier_semaphore()

    def greet(j, _):
        peer = lax.rem(me + j, slabs)
        pl.semaphore_signal(barrier, inc=1, device_id={"depth": peer}, device_id_type=MESH)
        return 0

    lax.fori_loop(1, slabs, greet, 0)

    first = jnp.concatenate([w1t[...].astype(F), jnp.zeros((96, 128), F)], axis=0)
    first = jnp.transpose(first).astype(BF)
    first = jnp.concatenate([first, jnp.zeros((128, 128), BF)], axis=1)
    channel = lax.broadcasted_iota(jnp.int32, (256, 128), 0)
    column = lax.broadcasted_iota(jnp.int32, (256, 128), 1)
    zero = jnp.zeros((128, 128), BF)
    for q in range(2):
        spread = jnp.concatenate(
            [(column == channel * 4 + (2 * q + k)).astype(F).astype(BF) for k in range(2)], axis=1
        )
        pltpu.matmul_push_rhs(spread, 0, q)
        pltpu.matmul_acc_lhs(accw[q], first, load_staged_rhs=0)
    for q in range(2):
        wide = pltpu.matmul_pop(accw[q]).astype(BF)
        for k in range(2):
            for j in range(2):
                w1p[j, q, k * 128 : (k + 1) * 128, j * 128 : (j + 1) * 128] = wide[:, k * 128 : (k + 1) * 128]
                w1p[j, q, k * 128 : (k + 1) * 128, (1 - j) * 128 : (2 - j) * 128] = zero
    for k in range(2):
        w2p[k * 128 : (k + 1) * 128, k * 128 : (k + 1) * 128] = w2[...]
        w2p[k * 128 : (k + 1) * 128, (1 - k) * 128 : (2 - k) * 128] = zero
    last = w3[...].astype(F)
    none = jnp.zeros((4, 128), F)
    for q in range(2):
        left = jnp.concatenate([last if s == 2 * q else none for s in range(4)], axis=0)
        right = jnp.concatenate([last if s == 2 * q + 1 else none for s in range(4)], axis=0)
        w3p[q] = jnp.concatenate([left, right], axis=1).astype(BF)
    bias[0] = jnp.transpose(jnp.broadcast_to(b1[...], (128, 128)))
    bias[1] = jnp.transpose(jnp.broadcast_to(b2[...], (128, 128)))
    flip = jnp.full((8, 128), order[0], jnp.int32) == 1
    b_last = [bl_ref[i] for i in range(4)]

    def prep(k, m, j):
        if m == 0 and j == 0:
            xcopy(k).wait()
        tile = xbuf[k, :, :, m * 512 + j * 256 : m * 512 + (j + 1) * 256]
        xs[lax.rem(k, 2), m, j * 128 : (j + 1) * 128, :] = tile.reshape(128, 256)

    def settle(acc, layer, i, dst, m):
        r = (i * CH) % 128
        shift = bias[layer, r : r + CH, :]
        value = pltpu.matmul_pop(acc) + jnp.concatenate([shift, shift], axis=1)
        dst[m, i * CH : (i + 1) * CH, :] = jnp.maximum(value.astype(BF), jnp.zeros((), BF))

    def push_x(par, stage):
        for m in range(2):
            pltpu.matmul_push_rhs(xs[par, m], stage, m)

    def push_h(h, stage):
        for m in range(2):
            pltpu.matmul_push_rhs(h[m], stage, m)

    def layer_one(u, stage, drain):
        j, q = UNITS[u]
        for i in range(NCH):
            for m in range(2):
                pltpu.matmul_acc_lhs(
                    acc1[m][i], w1p[j, q, i * CH : (i + 1) * CH, :], load_staged_rhs=stage if i == 0 else None
                )
                if drain:
                    settle(acc2[m][i], 1, i, h2s, m)

    def layer_two(stage, drain):
        for i in range(NCH):
            for m in range(2):
                pltpu.matmul_acc_lhs(
                    acc2[m][i], w2p[i * CH : (i + 1) * CH, :], load_staged_rhs=stage if i == 0 else None
                )
                if drain:
                    settle(acc1[m][i], 0, i, h1s, m)

    def layer_three(u, stage, par):
        j, q = UNITS[u]
        for m in range(2):
            pltpu.matmul_acc_lhs(acc3[m][j], w3p[q], load_staged_rhs=stage)
        if q == 1:
            for m in range(2):
                value = pltpu.matmul_pop(acc3[m][j])
                t = 2 * m + j
                z_ref[pl.ds(par * 128 + 32 * t, 16), :] = value[:, :128]
                z_ref[pl.ds(par * 128 + 32 * t + 16, 16), :] = value[:, 128:]

    def drain_two():
        for i in range(NCH):
            for m in range(2):
                settle(acc2[m][i], 1, i, h2s, m)

    def brick(k, is_first=False, is_last=False, extra=None):
        par = lax.rem(k, 2)
        for u in range(4):
            begins = is_first and u == 0
            ends = is_last and u == 3
            base = (u * 3) % 2
            push_h(h1s, 1 - base)
            if not ends:
                layer_one((u + 1) % 4, base, not begins)
            else:
                drain_two()
            if not is_last:
                prep(k + 1, u % 2, u // 2)
            if u == 2 and extra:
                extra()
            if not begins:
                push_h(h2s, base)
            layer_two(1 - base, not ends)
            if u < 2:
                push_x(par, 1 - base)
            elif not is_last:
                push_x(1 - par, 1 - base)
            if not begins:
                if u > 0:
                    layer_three(u - 1, base, par)
                else:
                    layer_three(3, base, 1 - par)

    def send(k, j):
        chunk = lax.rem(low + j, 8)
        return pltpu.make_async_remote_copy(
            src_ref=sent.at[k * 8 + chunk],
            dst_ref=taken.at[me],
            send_sem=send_sem,
            recv_sem=recv_sem,
            device_id={"depth": place(k) * 8 + chunk},
            device_id_type=MESH,
        )

    def finish(k):
        row = pl.multiple_of(place(k) * 8, 8)
        layers = stack_samples(z_ref, spans, lax.rem(k, 2) * 128, row, flip, b_last, spacing)
        for ch in range(4):
            sent[pl.ds(k * 8, 8), ch, :] = layers[ch]

    def finish_send(k):
        finish(k)
        for j in range(8):
            send(k, j).start()

    for m in range(2):
        for j in range(2):
            prep(0, m, j)
    push_x(0, 1)
    for i in range(NCH):
        for m in range(2):
            pltpu.matmul_acc_lhs(
                acc1[m][i], w1p[0, 0, i * CH : (i + 1) * CH, :], load_staged_rhs=1 if i == 0 else None
            )
    push_x(0, 0)
    for i in range(NCH):
        for m in range(2):
            settle(acc1[m][i], 0, i, h1s, m)
    brick(0, is_first=True)
    pl.semaphore_wait(barrier, slabs - 1)

    def step(k, _):
        brick(k, extra=lambda: finish_send(k - 1))
        return 0

    lax.fori_loop(1, bricks - 1, step, 0)
    brick(bricks - 1, is_last=True, extra=lambda: finish_send(bricks - 2))
    drain_two()
    push_h(h2s, 0)
    layer_three(3, 0, (bricks - 1) % 2)
    finish(bricks - 1)
    for j in range(1, 8):
        send(bricks - 1, j).start()
    taken[me] = sent[(bricks - 1) * 8 + low]

    others = pltpu.make_async_remote_copy(
        src_ref=sent.at[pl.ds(0, slabs - 1)],
        dst_ref=taken.at[pl.ds(0, slabs - 1)],
        send_sem=send_sem,
        recv_sem=recv_sem,
        device_id={"depth": lax.rem(me + 1, slabs)},
        device_id_type=MESH,
    )
    others.wait_recv()
    groups = [[taken[pl.ds(k, 8, stride=8), ch, :] for ch in range(4)] for k in range(8)]
    while len(groups) > 1:
        groups = [ordered(flip, a, b) for a, b in zip(groups[::2], groups[1::2])]
    total = groups[0]
    for shift in (7, 6, 4):
        total = ordered(flip, total, [pltpu.roll(c, shift, 0) for c in total])
    out[...] = jnp.concatenate([c[0:1] for c in total], axis=0)
    others.wait_send()


def per_device(features, ray_spans, view_order, w_first, b_first, w_second, b_second, w_last, b_last):
    slabs = lax.axis_size("depth")
    vmem = pl.BlockSpec(memory_space=pltpu.VMEM)
    smem = pl.BlockSpec(memory_space=pltpu.SMEM)
    return pl.pallas_call(
        functools.partial(kernel, slabs=slabs),
        out_shape=jax.ShapeDtypeStruct((4, 128), F),
        in_specs=[pl.BlockSpec(memory_space=pltpu.HBM), vmem, smem, vmem, vmem, vmem, vmem, vmem, smem],
        out_specs=vmem,
        scratch_shapes=[
            pltpu.VMEM((8, 32, 4, BRICK), BF),
            pltpu.VMEM((2, 2, 256, 256), BF),
            pltpu.VMEM((2, 2, 256, 256), BF),
            pltpu.VMEM((256, 256), BF),
            pltpu.VMEM((2, 16, 256), BF),
            pltpu.VMEM((2, 128, 128), F),
            pltpu.VMEM((2 * 8 * 16, 128), F),
            pltpu.VMEM((2, 256, 256), BF),
            pltpu.VMEM((2, 256, 256), BF),
            pltpu.VMEM((64, 4, 128), F),
            pltpu.VMEM((64, 4, 128), F),
            pltpu.SemaphoreType.DMA((8,)),
            pltpu.SemaphoreType.DMA,
            pltpu.SemaphoreType.DMA,
        ],
        compiler_params=pltpu.CompilerParams(
            collective_id=0, has_side_effects=True, vmem_limit_bytes=60 * 2**20
        ),
    )(
        features,
        ray_spans.reshape(2, 64, 128),
        view_order,
        w_first.T,
        w_second,
        w_last,
        b_first.reshape(1, 128),
        b_second.reshape(1, 128),
        b_last,
    )


def solution(mesh):
    return jax.shard_map(
        per_device,
        mesh=mesh,
        in_specs=(P(None, "depth", "tile"), P(None, "depth", "tile"), P("tile"), P(), P(), P(), P(), P(), P()),
        out_specs=P(None, ("tile", "depth")),
        check_vma=False,
    )
```

time: 109 us -> 37.7 us (0.35)
  the two profiles are of different devices: /device:TPU:2 before, /device:TPU:1 now
where the time goes in v1:
time: 37.7 us; the launch traced here: 37.5 us
  Pallas kernels  35.6 us (94%)
  local copies, waits for them, and re-layouts  1.26 us (3%)
  between operations  0.66 us (2%)
    pallas_call x1, Pallas kernels, per_device(): pl.pallas_call(functools.partial(kernel, slabs=slabs), out_shape=jax.Shap...  35.6 us
    unnamed x1, local copies, waits for them, and re-layouts  1.26 us

profile of v1, /device:TPU:1, one launch (start us, length us, event | category | flops | bytes accessed | tf_op | source)
XLA Modules:
  0.0 37.5 jit_solution(13563987179666653299)
XLA Ops:
  0.7 35.6 %shard_map.91 = f32[4,128]{1,0:T(4,128)} custom-call(bf16[32,4,8192]{2,1,0:T(4,128)(2,1)} %refs_0_.1, s32[2,64,128]{2,1,0:T(8,128)} %bitcast.4, s32[1]{0:T(128)S(6)} %copy.11.refs_2_, bf16[32,128]{1,0:T(8,128)(2,1)} %bitcast.5, bf16[128,128]{1,0:T(8,128)(2,1)} %refs_4_.1, bf16[4,128]{1,0:T(4,128)(2,1)} %refs_5_.1, f32[1,128]{1,0:T(1,128)} %bitcast.6, ...), custom_call_target="tpu_custom_call" | custom-call | tf_op jit(solution)/shard_map/pallas_call | solution.py:297
  36.3 1.3 %copy.12 = f32[4,128]{1,0:T(4,128)} copy(f32[4,128]{1,0:T(4,128)} %shard_map.91) | data formatting | bytes 4096

commit v2 on v1

--- a/solution.py
+++ b/solution.py
@@ -11,8 +11,6 @@
 F = jnp.float32
 BRICK = 1024
 CH = 32
-NCH = 256 // CH
-UNITS = ((0, 0), (0, 1), (1, 0), (1, 1))
 MESH = pl.DeviceIdType.MESH
 
 
@@ -64,8 +62,7 @@
 def kernel(*refs, slabs):
     accs = []
     for m in range(2):
-        accs += [pltpu.ACC(m)((CH, 256), F)] * (2 * NCH)
-        accs += [pltpu.ACC(m)((16, 256), F)] * 2 + [pltpu.ACC(m)((128, 256), F)]
+        accs += [pltpu.ACC(m)((CH, 256), F)] * 31 + [pltpu.ACC(m)((16, 256), F)] * 2
     pl.run_scoped(lambda *accs: body(*refs, accs=accs, slabs=slabs), *accs)
 
 
@@ -74,11 +71,9 @@
     xbuf, xs, w1p, w2p, w3p, bias, z_ref, h1s, h2s, sent, taken, sem, send_sem, recv_sem,
     *, accs, slabs,
 ):
-    n = 2 * NCH + 3
-    acc1 = [accs[m * n : m * n + NCH] for m in range(2)]
-    acc2 = [accs[m * n + NCH : m * n + 2 * NCH] for m in range(2)]
-    acc3 = [accs[m * n + 2 * NCH : m * n + 2 * NCH + 2] for m in range(2)]
-    accw = [accs[m * n + 2 * NCH + 2] for m in range(2)]
+    acc1 = [accs[m * 33 : m * 33 + 16] for m in range(2)]
+    acc2 = [accs[m * 33 + 16 : m * 33 + 31] + accs[m * 33 + 16 : m * 33 + 17] for m in range(2)]
+    acc3 = [accs[m * 33 + 31 : m * 33 + 33] for m in range(2)]
     bricks = 8
     me = lax.axis_index("depth")
     low = lax.rem(me, 8)
@@ -109,22 +104,25 @@
     first = jnp.concatenate([first, jnp.zeros((128, 128), BF)], axis=1)
     channel = lax.broadcasted_iota(jnp.int32, (256, 128), 0)
     column = lax.broadcasted_iota(jnp.int32, (256, 128), 1)
-    zero = jnp.zeros((128, 128), BF)
     for q in range(2):
         spread = jnp.concatenate(
             [(column == channel * 4 + (2 * q + k)).astype(F).astype(BF) for k in range(2)], axis=1
         )
         pltpu.matmul_push_rhs(spread, 0, q)
-        pltpu.matmul_acc_lhs(accw[q], first, load_staged_rhs=0)
+        for i in range(4):
+            rows = first[i * CH : (i + 1) * CH]
+            pltpu.matmul_acc_lhs(acc1[q][i], rows, load_staged_rhs=0 if i == 0 else None)
     for q in range(2):
-        wide = pltpu.matmul_pop(accw[q]).astype(BF)
-        for k in range(2):
-            for j in range(2):
-                w1p[j, q, k * 128 : (k + 1) * 128, j * 128 : (j + 1) * 128] = wide[:, k * 128 : (k + 1) * 128]
-                w1p[j, q, k * 128 : (k + 1) * 128, (1 - j) * 128 : (2 - j) * 128] = zero
+        for i in range(4):
+            wide = pltpu.matmul_pop(acc1[q][i]).astype(BF)
+            for k in range(2):
+                rows = pl.ds(q * 256 + k * 128 + i * CH, CH)
+                for j in range(2):
+                    w1p[j, rows, j * 128 : (j + 1) * 128] = wide[:, k * 128 : (k + 1) * 128]
+                    w1p[j, rows, (1 - j) * 128 : (2 - j) * 128] = jnp.zeros((CH, 128), BF)
     for k in range(2):
         w2p[k * 128 : (k + 1) * 128, k * 128 : (k + 1) * 128] = w2[...]
-        w2p[k * 128 : (k + 1) * 128, (1 - k) * 128 : (2 - k) * 128] = zero
+        w2p[k * 128 : (k + 1) * 128, (1 - k) * 128 : (2 - k) * 128] = jnp.zeros((128, 128), BF)
     last = w3[...].astype(F)
     none = jnp.zeros((4, 128), F)
     for q in range(2):
@@ -136,88 +134,87 @@
     flip = jnp.full((8, 128), order[0], jnp.int32) == 1
     b_last = [bl_ref[i] for i in range(4)]
 
-    def prep(k, m, j):
-        if m == 0 and j == 0:
-            xcopy(k).wait()
-        tile = xbuf[k, :, :, m * 512 + j * 256 : m * 512 + (j + 1) * 256]
-        xs[lax.rem(k, 2), m, j * 128 : (j + 1) * 128, :] = tile.reshape(128, 256)
-
-    def settle(acc, layer, i, dst, m):
+    def prep(k):
+        for m in range(2):
+            for j in range(2):
+                tile = xbuf[k, :, :, m * 512 + j * 256 : m * 512 + (j + 1) * 256]
+                xs[lax.rem(k, 2), m, j * 128 : (j + 1) * 128, :] = tile.reshape(128, 256)
+
+    def push(source, stage):
+        for m in range(2):
+            pltpu.matmul_push_rhs(source(m), stage, m)
+
+    def mm1(j, i, stage):
+        for m in range(2):
+            rows = w1p[j, i * CH : (i + 1) * CH, :]
+            pltpu.matmul_acc_lhs(acc1[m][i], rows, load_staged_rhs=stage if i == 0 else None)
+
+    def mm2(i, stage):
+        for m in range(2):
+            rows = w2p[(i % 8) * CH : (i % 8 + 1) * CH, :]
+            pltpu.matmul_acc_lhs(acc2[m][i], rows, load_staged_rhs=stage if i % 8 == 0 else None)
+
+    def mm3(j, q, stage):
+        for m in range(2):
+            pltpu.matmul_acc_lhs(acc3[m][j], w3p[q], load_staged_rhs=stage)
+
+    def settle(acc, layer, i, dst):
         r = (i * CH) % 128
         shift = bias[layer, r : r + CH, :]
-        value = pltpu.matmul_pop(acc) + jnp.concatenate([shift, shift], axis=1)
-        dst[m, i * CH : (i + 1) * CH, :] = jnp.maximum(value.astype(BF), jnp.zeros((), BF))
-
-    def push_x(par, stage):
-        for m in range(2):
-            pltpu.matmul_push_rhs(xs[par, m], stage, m)
-
-    def push_h(h, stage):
-        for m in range(2):
-            pltpu.matmul_push_rhs(h[m], stage, m)
-
-    def layer_one(u, stage, drain):
-        j, q = UNITS[u]
-        for i in range(NCH):
-            for m in range(2):
-                pltpu.matmul_acc_lhs(
-                    acc1[m][i], w1p[j, q, i * CH : (i + 1) * CH, :], load_staged_rhs=stage if i == 0 else None
-                )
-                if drain:
-                    settle(acc2[m][i], 1, i, h2s, m)
-
-    def layer_two(stage, drain):
-        for i in range(NCH):
-            for m in range(2):
-                pltpu.matmul_acc_lhs(
-                    acc2[m][i], w2p[i * CH : (i + 1) * CH, :], load_staged_rhs=stage if i == 0 else None
-                )
-                if drain:
-                    settle(acc1[m][i], 0, i, h1s, m)
-
-    def layer_three(u, stage, par):
-        j, q = UNITS[u]
-        for m in range(2):
-            pltpu.matmul_acc_lhs(acc3[m][j], w3p[q], load_staged_rhs=stage)
-        if q == 1:
-            for m in range(2):
-                value = pltpu.matmul_pop(acc3[m][j])
-                t = 2 * m + j
-                z_ref[pl.ds(par * 128 + 32 * t, 16), :] = value[:, :128]
-                z_ref[pl.ds(par * 128 + 32 * t + 16, 16), :] = value[:, 128:]
-
-    def drain_two():
-        for i in range(NCH):
-            for m in range(2):
-                settle(acc2[m][i], 1, i, h2s, m)
-
-    def brick(k, is_first=False, is_last=False, extra=None):
+        shift = jnp.concatenate([shift, shift], axis=1)
+        for m in range(2):
+            value = (pltpu.matmul_pop(acc[m][i]) + shift).astype(BF)
+            dst[m, i * CH : (i + 1) * CH, :] = jnp.maximum(value, jnp.zeros((), BF))
+
+    def pop3(j, par):
+        for m in range(2):
+            value = pltpu.matmul_pop(acc3[m][j])
+            row = par * 128 + 32 * (2 * m + j)
+            z_ref[pl.ds(row, 16), :] = value[:, :128]
+            z_ref[pl.ds(row + 16, 16), :] = value[:, 128:]
+
+    def slot(k, j, first=False, second=False, last=False, last_brick=False, middle=None, late=None):
         par = lax.rem(k, 2)
-        for u in range(4):
-            begins = is_first and u == 0
-            ends = is_last and u == 3
-            base = (u * 3) % 2
-            push_h(h1s, 1 - base)
-            if not ends:
-                layer_one((u + 1) % 4, base, not begins)
-            else:
-                drain_two()
-            if not is_last:
-                prep(k + 1, u % 2, u // 2)
-            if u == 2 and extra:
-                extra()
-            if not begins:
-                push_h(h2s, base)
-            layer_two(1 - base, not ends)
-            if u < 2:
-                push_x(par, 1 - base)
-            elif not is_last:
-                push_x(1 - par, 1 - base)
-            if not begins:
-                if u > 0:
-                    layer_three(u - 1, base, par)
-                else:
-                    layer_three(3, base, 1 - par)
+        s0, s1 = j % 2, 1 - j % 2
+        push(lambda m: h1s[m, 0:256, :], s1)
+        for i in range(16):
+            if not last:
+                mm1(1 - j, i, s0)
+            if i >= 1 and not first:
+                settle(acc2, 1, i, h2s)
+            if i == 8 and not first:
+                push(lambda m: h2s[m, 0:256, :], s0)
+        if middle:
+            middle()
+        if not first and not second:
+            pop3(j, 1 - par)
+        for i in range(8):
+            mm2(i, s1)
+            if not last:
+                settle(acc1, 0, i, h1s)
+        push(lambda m: h1s[m, 256:512, :], s1)
+        if not first:
+            mm3(1 - j, 0, s0)
+            push(lambda m: h2s[m, 256:512, :], s0)
+        for i in range(8, 16):
+            if i == 15:
+                settle(acc2, 1, 0, h2s)
+            mm2(i, s1)
+            if not last:
+                settle(acc1, 0, i, h1s)
+        if late:
+            late()
+        if not last_brick:
+            push(lambda m: xs[1 - par, m], s1)
+        if not first:
+            mm3(1 - j, 1, s0)
+
+    def brick(k, first=False, last=False, late=None):
+        if not last:
+            xcopy(k + 1).wait()
+        middle = None if last else lambda: prep(k + 1)
+        slot(k, 0, first=first, last_brick=last, middle=middle)
+        slot(k, 1, second=first, last=last, last_brick=last, late=late)
 
     def send(k, j):
         chunk = lax.rem(low + j, 8)
@@ -241,31 +238,31 @@
         for j in range(8):
             send(k, j).start()
 
-    for m in range(2):
-        for j in range(2):
-            prep(0, m, j)
-    push_x(0, 1)
-    for i in range(NCH):
-        for m in range(2):
-            pltpu.matmul_acc_lhs(
-                acc1[m][i], w1p[0, 0, i * CH : (i + 1) * CH, :], load_staged_rhs=1 if i == 0 else None
-            )
-    push_x(0, 0)
-    for i in range(NCH):
-        for m in range(2):
-            settle(acc1[m][i], 0, i, h1s, m)
-    brick(0, is_first=True)
+    xcopy(0).wait()
+    prep(0)
+    push(lambda m: xs[0, m], 1)
+    for i in range(16):
+        mm1(0, i, 1)
+    push(lambda m: xs[0, m], 0)
+    for i in range(16):
+        settle(acc1, 0, i, h1s)
+    brick(0, first=True)
     pl.semaphore_wait(barrier, slabs - 1)
 
     def step(k, _):
-        brick(k, extra=lambda: finish_send(k - 1))
+        brick(k, late=lambda: finish_send(k - 1))
         return 0
 
     lax.fori_loop(1, bricks - 1, step, 0)
-    brick(bricks - 1, is_last=True, extra=lambda: finish_send(bricks - 2))
-    drain_two()
-    push_h(h2s, 0)
-    layer_three(3, 0, (bricks - 1) % 2)
+    brick(bricks - 1, last=True, late=lambda: finish_send(bricks - 2))
+    for i in range(1, 16):
+        settle(acc2, 1, i, h2s)
+    push(lambda m: h2s[m, 0:256, :], 0)
+    push(lambda m: h2s[m, 256:512, :], 1)
+    pop3(0, (bricks - 1) % 2)
+    mm3(1, 0, 0)
+    mm3(1, 1, 1)
+    pop3(1, (bricks - 1) % 2)
     finish(bricks - 1)
     for j in range(1, 8):
         send(bricks - 1, j).start()
@@ -302,13 +299,13 @@
         scratch_shapes=[
             pltpu.VMEM((8, 32, 4, BRICK), BF),
             pltpu.VMEM((2, 2, 256, 256), BF),
-            pltpu.VMEM((2, 2, 256, 256), BF),
+            pltpu.VMEM((2, 512, 256), BF),
             pltpu.VMEM((256, 256), BF),
             pltpu.VMEM((2, 16, 256), BF),
             pltpu.VMEM((2, 128, 128), F),
             pltpu.VMEM((2 * 8 * 16, 128), F),
-            pltpu.VMEM((2, 256, 256), BF),
-            pltpu.VMEM((2, 256, 256), BF),
+            pltpu.VMEM((2, 512, 256), BF),
+            pltpu.VMEM((2, 512, 256), BF),
             pltpu.VMEM((64, 4, 128), F),
             pltpu.VMEM((64, 4, 128), F),
             pltpu.SemaphoreType.DMA((8,)),

time: 37.7 us -> 35.9 us (0.952)
  Pallas kernels: 35.6 us -> 33.7 us
    pallas_call x1, Pallas kernels: 35.6 us -> 33.7 us  [per_device(): pl.pallas_call(functools.partial(kernel, slabs=slabs), out_shape=jax.Shap...]
where the time goes in v2:
time: 35.9 us; the launch traced here: 35.7 us
  Pallas kernels  33.7 us (94%)
  local copies, waits for them, and re-layouts  1.26 us (4%)
  between operations  0.66 us (2%)
    pallas_call x1, Pallas kernels, per_device(): pl.pallas_call(functools.partial(kernel, slabs=slabs), out_shape=jax.Shap...  33.7 us
    unnamed x1, local copies, waits for them, and re-layouts  1.26 us

profile of v2, /device:TPU:1, one launch (start us, length us, event | category | flops | bytes accessed | tf_op | source)
XLA Modules:
  0.0 35.7 jit_solution(10622247817626288651)
XLA Ops:
  0.7 33.7 %shard_map.91 = f32[4,128]{1,0:T(4,128)} custom-call(bf16[32,4,8192]{2,1,0:T(4,128)(2,1)} %refs_0_.1, s32[2,64,128]{2,1,0:T(8,128)} %bitcast.4, s32[1]{0:T(128)S(6)} %copy.11.refs_2_, bf16[32,128]{1,0:T(8,128)(2,1)} %bitcast.5, bf16[128,128]{1,0:T(8,128)(2,1)} %refs_4_.1, bf16[4,128]{1,0:T(4,128)(2,1)} %refs_5_.1, f32[1,128]{1,0:T(1,128)} %bitcast.6, ...), custom_call_target="tpu_custom_call" | custom-call | tf_op jit(solution)/shard_map/pallas_call | solution.py:294
  34.4 1.3 %copy.12 = f32[4,128]{1,0:T(4,128)} copy(f32[4,128]{1,0:T(4,128)} %shard_map.91) | data formatting | bytes 4096

commit v3 on v2

--- a/solution.py
+++ b/solution.py
@@ -12,6 +12,11 @@
 BRICK = 1024
 CH = 32
 MESH = pl.DeviceIdType.MESH
+AWAY = (4, 3, 5, 2, 6, 1, 7, 0)
+PEERS = sorted(
+    ((a, b) for a in range(8) for b in range(8) if a or b),
+    key=lambda p: -(min(p[0], 8 - p[0]) + min(p[1], 8 - p[1])),
+)
 
 
 def over(near, far):
@@ -67,8 +72,9 @@
 
 
 def body(
-    x_hbm, spans, order, w1t, w2, w3, b1, b2, bl_ref, out,
-    xbuf, xs, w1p, w2p, w3p, bias, z_ref, h1s, h2s, sent, taken, sem, send_sem, recv_sem,
+    x_hbm, spans_hbm, order, w1_hbm, w2_hbm, w3_hbm, b1_hbm, b2_hbm, bl_hbm, out,
+    xbuf, xs, w1p, w2p, w3p, bias, z_ref, h1s, h2s, sent, taken,
+    spans, w1t, w2, w3, b1, b2, bl, sem, small_sem, send_sem, recv_sem,
     *, accs, slabs,
 ):
     acc1 = [accs[m * 33 : m * 33 + 16] for m in range(2)]
@@ -80,24 +86,38 @@
     high = lax.div(me, 8)
     spacing = 6.0 / (4 * slabs)
 
+    barrier = pltpu.get_barrier_semaphore()
+    for dx, dz in PEERS:
+        peer = lax.rem(high + dx, 8) * 8 + lax.rem(low + dz, 8)
+        pl.semaphore_signal(barrier, inc=1, device_id={"depth": peer}, device_id_type=MESH)
+
     def place(k):
-        return lax.rem(high + 1 + k, 8)
+        step = lax.div(k + 1, 2)
+        away = jnp.where(lax.rem(k, 2) == 1, 4 - step, 4 + step)
+        return lax.rem(high + lax.rem(away, 8), 8)
 
     def xcopy(k):
         start = pl.multiple_of(place(k) * BRICK, BRICK)
         return pltpu.make_async_copy(x_hbm.at[:, :, pl.ds(start, BRICK)], xbuf.at[k], sem.at[k])
 
-    for k in range(bricks):
+    small = [
+        pltpu.make_async_copy(src, dst, small_sem.at[i])
+        for i, (src, dst) in enumerate(
+            (
+                (w1_hbm, w1t), (w2_hbm, w2), (w3_hbm, w3), (b1_hbm, b1), (b2_hbm, b2),
+                (bl_hbm, bl), (spans_hbm, spans),
+            )
+        )
+    ]
+    for copy in small[:1]:
+        copy.start()
+    xcopy(0).start()
+    for copy in small[1:]:
+        copy.start()
+    for k in range(1, bricks):
         xcopy(k).start()
-
-    barrier = pltpu.get_barrier_semaphore()
-
-    def greet(j, _):
-        peer = lax.rem(me + j, slabs)
-        pl.semaphore_signal(barrier, inc=1, device_id={"depth": peer}, device_id_type=MESH)
-        return 0
-
-    lax.fori_loop(1, slabs, greet, 0)
+    for copy in small:
+        copy.wait()
 
     first = jnp.concatenate([w1t[...].astype(F), jnp.zeros((96, 128), F)], axis=0)
     first = jnp.transpose(first).astype(BF)
@@ -132,7 +152,7 @@
     bias[0] = jnp.transpose(jnp.broadcast_to(b1[...], (128, 128)))
     bias[1] = jnp.transpose(jnp.broadcast_to(b2[...], (128, 128)))
     flip = jnp.full((8, 128), order[0], jnp.int32) == 1
-    b_last = [bl_ref[i] for i in range(4)]
+    b_last = [jnp.broadcast_to(bl[0:1, i : i + 1], (8, 128)) for i in range(4)]
 
     def prep(k):
         for m in range(2):
@@ -217,7 +237,7 @@
         slot(k, 1, second=first, last=last, last_brick=last, late=late)
 
     def send(k, j):
-        chunk = lax.rem(low + j, 8)
+        chunk = lax.rem(low + AWAY[j], 8)
         return pltpu.make_async_remote_copy(
             src_ref=sent.at[k * 8 + chunk],
             dst_ref=taken.at[me],
@@ -233,8 +253,7 @@
         for ch in range(4):
             sent[pl.ds(k * 8, 8), ch, :] = layers[ch]
 
-    def finish_send(k):
-        finish(k)
+    def send_brick(k):
         for j in range(8):
             send(k, j).start()
 
@@ -247,14 +266,24 @@
     for i in range(16):
         settle(acc1, 0, i, h1s)
     brick(0, first=True)
-    pl.semaphore_wait(barrier, slabs - 1)
 
     def step(k, _):
-        brick(k, late=lambda: finish_send(k - 1))
+        brick(k, late=lambda: finish(k - 1))
+
+        @pl.when(k == 2)
+        def _():
+            pl.semaphore_wait(barrier, slabs - 1)
+            send_brick(0)
+
+        @pl.when(k >= 2)
+        def _():
+            send_brick(k - 1)
+
         return 0
 
     lax.fori_loop(1, bricks - 1, step, 0)
-    brick(bricks - 1, last=True, late=lambda: finish_send(bricks - 2))
+    brick(bricks - 1, last=True, late=lambda: finish(bricks - 2))
+    send_brick(bricks - 2)
     for i in range(1, 16):
         settle(acc2, 1, i, h2s)
     push(lambda m: h2s[m, 0:256, :], 0)
@@ -264,7 +293,7 @@
     mm3(1, 1, 1)
     pop3(1, (bricks - 1) % 2)
     finish(bricks - 1)
-    for j in range(1, 8):
+    for j in range(7):
         send(bricks - 1, j).start()
     taken[me] = sent[(bricks - 1) * 8 + low]
 
@@ -289,13 +318,12 @@
 
 def per_device(features, ray_spans, view_order, w_first, b_first, w_second, b_second, w_last, b_last):
     slabs = lax.axis_size("depth")
-    vmem = pl.BlockSpec(memory_space=pltpu.VMEM)
-    smem = pl.BlockSpec(memory_space=pltpu.SMEM)
+    hbm = pl.BlockSpec(memory_space=pltpu.HBM)
     return pl.pallas_call(
         functools.partial(kernel, slabs=slabs),
         out_shape=jax.ShapeDtypeStruct((4, 128), F),
-        in_specs=[pl.BlockSpec(memory_space=pltpu.HBM), vmem, smem, vmem, vmem, vmem, vmem, vmem, smem],
-        out_specs=vmem,
+        in_specs=[hbm, hbm, pl.BlockSpec(memory_space=pltpu.SMEM)] + [hbm] * 6,
+        out_specs=pl.BlockSpec(memory_space=pltpu.VMEM),
         scratch_shapes=[
             pltpu.VMEM((8, 32, 4, BRICK), BF),
             pltpu.VMEM((2, 2, 256, 256), BF),
@@ -308,7 +336,15 @@
             pltpu.VMEM((2, 512, 256), BF),
             pltpu.VMEM((64, 4, 128), F),
             pltpu.VMEM((64, 4, 128), F),
+            pltpu.VMEM((2, 64, 128), jnp.int32),
+            pltpu.VMEM((32, 128), BF),
+            pltpu.VMEM((128, 128), BF),
+            pltpu.VMEM((4, 128), BF),
+            pltpu.VMEM((1, 128), F),
+            pltpu.VMEM((1, 128), F),
+            pltpu.VMEM((1, 4), F),
             pltpu.SemaphoreType.DMA((8,)),
+            pltpu.SemaphoreType.DMA((7,)),
             pltpu.SemaphoreType.DMA,
             pltpu.SemaphoreType.DMA,
         ],
@@ -324,7 +360,7 @@
         w_last,
         b_first.reshape(1, 128),
         b_second.reshape(1, 128),
-        b_last,
+        b_last.reshape(1, 4),
     )
 
 

time: 35.9 us -> 32.8 us (0.914)
  Pallas kernels: 33.7 us -> 30.7 us
    pallas_call x1, Pallas kernels: 33.7 us -> 30.7 us  [per_device(): pl.pallas_call(functools.partial(kernel, slabs=slabs), out_shape=jax.Shap...]
where the time goes in v3:
time: 32.8 us; the launch traced here: 32.6 us
  Pallas kernels  30.7 us (94%)
  local copies, waits for them, and re-layouts  1.26 us (4%)
  between operations  0.66 us (2%)
    pallas_call x1, Pallas kernels, per_device(): pl.pallas_call(functools.partial(kernel, slabs=slabs), out_shape=jax.Shap...  30.7 us
    unnamed x1, local copies, waits for them, and re-layouts  1.26 us

profile of v3, /device:TPU:1, one launch (start us, length us, event | category | flops | bytes accessed | tf_op | source)
XLA Modules:
  0.0 32.6 jit_solution(8702897882133422360)
XLA Ops:
  0.7 30.7 %shard_map.91 = f32[4,128]{1,0:T(4,128)} custom-call(bf16[32,4,8192]{2,1,0:T(4,128)(2,1)} %refs_0_.1, s32[2,64,128]{2,1,0:T(8,128)} %bitcast.5, s32[1]{0:T(128)S(6)} %copy.11.refs_2_, bf16[32,128]{1,0:T(8,128)(2,1)} %bitcast.6, bf16[128,128]{1,0:T(8,128)(2,1)} %refs_4_.1, bf16[4,128]{1,0:T(4,128)(2,1)} %refs_5_.1, f32[1,128]{1,0:T(1,128)} %bitcast.7, ...), custom_call_target="tpu_custom_call" | custom-call | tf_op jit(solution)/shard_map/pallas_call | solution.py:322
  31.3 1.3 %copy.12 = f32[4,128]{1,0:T(4,128)} copy(f32[4,128]{1,0:T(4,128)} %shard_map.91) | data formatting | bytes 4096

commit v4 on v3

--- a/solution.py
+++ b/solution.py
@@ -349,18 +349,20 @@
             pltpu.SemaphoreType.DMA,
         ],
         compiler_params=pltpu.CompilerParams(
-            collective_id=0, has_side_effects=True, vmem_limit_bytes=60 * 2**20
+            collective_id=0, has_side_effects=True, vmem_limit_bytes=40 * 2**20
         ),
     )(
-        features,
-        ray_spans.reshape(2, 64, 128),
+        *(
+            pltpu.with_memory_space_constraint(operand, pltpu.HBM)
+            for operand in (features, ray_spans.reshape(2, 64, 128))
+        ),
         view_order,
-        w_first.T,
-        w_second,
-        w_last,
-        b_first.reshape(1, 128),
-        b_second.reshape(1, 128),
-        b_last.reshape(1, 4),
+        *(
+            pltpu.with_memory_space_constraint(operand, pltpu.HBM)
+            for operand in (
+                w_first.T, w_second, w_last, b_first.reshape(1, 128), b_second.reshape(1, 128), b_last.reshape(1, 4)
+            )
+        ),
     )
 
 

time: 32.8 us -> 31.5 us (0.960)
  local copies, waits for them, and re-layouts: 1.26 us -> 0.58 us
  Pallas kernels: 30.7 us -> 30.1 us
    unnamed x1, local copies, waits for them, and re-layouts: 1.26 us -> 0.58 us
    pallas_call x1, Pallas kernels: 30.7 us -> 30.1 us  [per_device(): pl.pallas_call(functools.partial(kernel, slabs=slabs), out_shape=jax.Shap...]
where the time goes in v4:
time: 31.5 us; the launch traced here: 31.3 us
  Pallas kernels  30.1 us (96%)
  between operations  0.66 us (2%)
  local copies, waits for them, and re-layouts  0.58 us (2%)
    pallas_call x1, Pallas kernels, per_device(): pl.pallas_call(functools.partial(kernel, slabs=slabs), out_shape=jax.Shap...  30.1 us

profile of v4, /device:TPU:1, one launch (start us, length us, event | category | flops | bytes accessed | tf_op | source)
XLA Modules:
  0.0 31.3 jit_solution(9066036058939964865)
XLA Ops:
  0.7 30.1 %shard_map.91 = f32[4,128]{1,0:T(4,128)S(1)} custom-call(bf16[32,4,8192]{2,1,0:T(4,128)(2,1)} %refs_0_.1, s32[2,64,128]{2,1,0:T(8,128)} %bitcast.5, s32[1]{0:T(128)S(6)} %copy.11.refs_2_, bf16[32,128]{1,0:T(8,128)(2,1)} %bitcast.6, bf16[128,128]{1,0:T(8,128)(2,1)} %refs_4_.1, bf16[4,128]{1,0:T(4,128)(2,1)} %refs_5_.1, f32[1,128]{1,0:T(1,128)} %bitcast.7, ...), custom_call_target="tpu_custom_call" | custom-call | tf_op jit(solution)/shard_map/pallas_call | solution.py:322
  30.8 0.6 %copy.12 = f32[4,128]{1,0:T(4,128)} copy(f32[4,128]{1,0:T(4,128)S(1)} %shard_map.91) | data formatting | bytes 4096

commit v5 on v4

--- a/solution.py
+++ b/solution.py
@@ -13,10 +13,11 @@
 CH = 32
 MESH = pl.DeviceIdType.MESH
 AWAY = (4, 3, 5, 2, 6, 1, 7, 0)
+RING = tuple(min(a, 8 - a) for a in range(8))
 PEERS = sorted(
-    ((a, b) for a in range(8) for b in range(8) if a or b),
-    key=lambda p: -(min(p[0], 8 - p[0]) + min(p[1], 8 - p[1])),
+    ((a, b) for a in range(8) for b in range(8) if a or b), key=lambda p: -(RING[p[0]] + RING[p[1]])
 )
+FAR = [(a, b) for a, b in PEERS if RING[a] + RING[b] >= 6]
 
 
 def over(near, far):
@@ -74,7 +75,7 @@
 def body(
     x_hbm, spans_hbm, order, w1_hbm, w2_hbm, w3_hbm, b1_hbm, b2_hbm, bl_hbm, out,
     xbuf, xs, w1p, w2p, w3p, bias, z_ref, h1s, h2s, sent, taken,
-    spans, w1t, w2, w3, b1, b2, bl, sem, small_sem, send_sem, recv_sem,
+    spans, w1t, w2, w3, b1, b2, bl, sem, small_sem, send_sem, hand_sem, recv_sem,
     *, accs, slabs,
 ):
     acc1 = [accs[m * 33 : m * 33 + 16] for m in range(2)]
@@ -87,9 +88,23 @@
     spacing = 6.0 / (4 * slabs)
 
     barrier = pltpu.get_barrier_semaphore()
-    for dx, dz in PEERS:
+
+    def greet(dx, dz):
         peer = lax.rem(high + dx, 8) * 8 + lax.rem(low + dz, 8)
         pl.semaphore_signal(barrier, inc=1, device_id={"depth": peer}, device_id_type=MESH)
+
+    @pl.when(low < 6)
+    def _():
+        for dx, dz in FAR:
+            greet(dx, dz)
+
+    for dx, dz in PEERS:
+        if (dx, dz) not in FAR:
+            greet(dx, dz)
+
+    by_relay = jnp.where(
+        (low == 2) | (low == 3), 8, jnp.where((low == 1) | (low == 4), 4, jnp.where((low == 0) | (low == 5), 1, 0))
+    )
 
     def place(k):
         step = lax.div(k + 1, 2)
@@ -238,14 +253,43 @@
 
     def send(k, j):
         chunk = lax.rem(low + AWAY[j], 8)
+        owner = place(k) * 8 + chunk
+        way, target = 0, owner
+        if RING[AWAY[j]] >= 2:
+            far = (chunk >= 6) & (4 - lax.div(k + 1, 2) >= 6 - RING[AWAY[j]])
+            way = jnp.where(far, 8 - chunk, 0)
+            target = jnp.where(far, place(k) * 8, owner)
         return pltpu.make_async_remote_copy(
             src_ref=sent.at[k * 8 + chunk],
-            dst_ref=taken.at[me],
+            dst_ref=taken.at[way, me],
             send_sem=send_sem,
-            recv_sem=recv_sem,
-            device_id={"depth": place(k) * 8 + chunk},
+            recv_sem=recv_sem.at[way],
+            device_id={"depth": target},
             device_id_type=MESH,
         )
+
+    def arrived(way, count):
+        pltpu.make_async_remote_copy(
+            src_ref=sent.at[pl.ds(0, count)],
+            dst_ref=taken.at[0, pl.ds(0, count)],
+            send_sem=send_sem,
+            recv_sem=recv_sem.at[way],
+            device_id={"depth": lax.rem(me + 1, slabs)},
+            device_id_type=MESH,
+        ).wait_recv()
+
+    def hand_on(way):
+        arrived(way, len(FAR))
+        for dx, dz in FAR:
+            source = lax.rem(high + 8 - dx, 8) * 8 + (16 - way - dz) % 8
+            pltpu.make_async_remote_copy(
+                src_ref=taken.at[way, source],
+                dst_ref=taken.at[0, source],
+                send_sem=hand_sem,
+                recv_sem=recv_sem.at[3],
+                device_id={"depth": high * 8 + 8 - way},
+                device_id_type=MESH,
+            ).start()
 
     def finish(k):
         row = pl.multiple_of(place(k) * 8, 8)
@@ -270,12 +314,13 @@
     def step(k, _):
         brick(k, late=lambda: finish(k - 1))
 
-        @pl.when(k == 2)
+        @pl.when(k == 3)
         def _():
-            pl.semaphore_wait(barrier, slabs - 1)
+            pl.semaphore_wait(barrier, slabs - 1 - by_relay)
             send_brick(0)
-
-        @pl.when(k >= 2)
+            send_brick(1)
+
+        @pl.when(k >= 3)
         def _():
             send_brick(k - 1)
 
@@ -295,25 +340,48 @@
     finish(bricks - 1)
     for j in range(7):
         send(bricks - 1, j).start()
-    taken[me] = sent[(bricks - 1) * 8 + low]
-
-    others = pltpu.make_async_remote_copy(
-        src_ref=sent.at[pl.ds(0, slabs - 1)],
-        dst_ref=taken.at[pl.ds(0, slabs - 1)],
-        send_sem=send_sem,
-        recv_sem=recv_sem,
-        device_id={"depth": lax.rem(me + 1, slabs)},
-        device_id_type=MESH,
-    )
-    others.wait_recv()
-    groups = [[taken[pl.ds(k, 8, stride=8), ch, :] for ch in range(4)] for k in range(8)]
+    taken[0, me] = sent[(bricks - 1) * 8 + low]
+
+    @pl.when(low == 0)
+    def _():
+        hand_on(2)
+        hand_on(1)
+
+    @pl.when(low < 6)
+    def _():
+        arrived(0, slabs - 1)
+
+    @pl.when(low >= 6)
+    def _():
+        arrived(0, slabs - 1 - len(FAR))
+        arrived(3, len(FAR))
+
+    groups = [[taken[0, pl.ds(k, 8, stride=8), ch, :] for ch in range(4)] for k in range(8)]
     while len(groups) > 1:
         groups = [ordered(flip, a, b) for a, b in zip(groups[::2], groups[1::2])]
     total = groups[0]
     for shift in (7, 6, 4):
         total = ordered(flip, total, [pltpu.roll(c, shift, 0) for c in total])
     out[...] = jnp.concatenate([c[0:1] for c in total], axis=0)
-    others.wait_send()
+    pltpu.make_async_remote_copy(
+        src_ref=sent.at[pl.ds(0, slabs - 1)],
+        dst_ref=taken.at[0, pl.ds(0, slabs - 1)],
+        send_sem=send_sem,
+        recv_sem=recv_sem.at[0],
+        device_id={"depth": lax.rem(me + 1, slabs)},
+        device_id_type=MESH,
+    ).wait_send()
+
+    @pl.when(low == 0)
+    def _():
+        pltpu.make_async_remote_copy(
+            src_ref=sent.at[pl.ds(0, 2 * len(FAR))],
+            dst_ref=taken.at[0, pl.ds(0, 2 * len(FAR))],
+            send_sem=hand_sem,
+            recv_sem=recv_sem.at[3],
+            device_id={"depth": lax.rem(me + 1, slabs)},
+            device_id_type=MESH,
+        ).wait_send()
 
 
 def per_device(features, ray_spans, view_order, w_first, b_first, w_second, b_second, w_last, b_last):
@@ -335,7 +403,7 @@
             pltpu.VMEM((2, 512, 256), BF),
             pltpu.VMEM((2, 512, 256), BF),
             pltpu.VMEM((64, 4, 128), F),
-            pltpu.VMEM((64, 4, 128), F),
+            pltpu.VMEM((3, 64, 4, 128), F),
             pltpu.VMEM((2, 64, 128), jnp.int32),
             pltpu.VMEM((32, 128), BF),
             pltpu.VMEM((128, 128), BF),
@@ -347,6 +415,7 @@
             pltpu.SemaphoreType.DMA((7,)),
             pltpu.SemaphoreType.DMA,
             pltpu.SemaphoreType.DMA,
+            pltpu.SemaphoreType.DMA((4,)),
         ],
         compiler_params=pltpu.CompilerParams(
             collective_id=0, has_side_effects=True, vmem_limit_bytes=40 * 2**20

time: 31.5 us -> 30.5 us (0.968); the launches traced: 31.3 us -> 30 us
  Pallas kernels: 30.1 us -> 28.8 us
    pallas_call x1, Pallas kernels: 30.1 us -> 28.8 us  [per_device(): pl.pallas_call(functools.partial(kernel, slabs=slabs), out_shape=jax.Shap...]
where the time goes in v5:
time: 30.5 us; the launch traced here: 30 us
  Pallas kernels  28.8 us (94%)
  between operations  0.66 us (2%)
  local copies, waits for them, and re-layouts  0.58 us (2%)
    pallas_call x1, Pallas kernels, per_device(): pl.pallas_call(functools.partial(kernel, slabs=slabs), out_shape=jax.Shap...  28.8 us

profile of v5, /device:TPU:1, one launch (start us, length us, event | category | flops | bytes accessed | tf_op | source)
XLA Modules:
  0.0 30.0 jit_solution(6641877288870523894)
XLA Ops:
  0.7 28.8 %shard_map.91 = f32[4,128]{1,0:T(4,128)S(1)} custom-call(bf16[32,4,8192]{2,1,0:T(4,128)(2,1)} %refs_0_.1, s32[2,64,128]{2,1,0:T(8,128)} %bitcast.5, s32[1]{0:T(128)S(6)} %copy.11.refs_2_, bf16[32,128]{1,0:T(8,128)(2,1)} %bitcast.6, bf16[128,128]{1,0:T(8,128)(2,1)} %refs_4_.1, bf16[4,128]{1,0:T(4,128)(2,1)} %refs_5_.1, f32[1,128]{1,0:T(1,128)} %bitcast.7, ...), custom_call_target="tpu_custom_call" | custom-call | tf_op jit(solution)/shard_map/pallas_call | solution.py:390
  29.4 0.6 %copy.12 = f32[4,128]{1,0:T(4,128)} copy(f32[4,128]{1,0:T(4,128)S(1)} %shard_map.91) | data formatting | bytes 4096

commit v6 on v5

--- a/solution.py
+++ b/solution.py
@@ -85,6 +85,7 @@
     me = lax.axis_index("depth")
     low = lax.rem(me, 8)
     high = lax.div(me, 8)
+    mirrored = lax.rem(lax.axis_index("tile"), 2) == 1
     spacing = 6.0 / (4 * slabs)
 
     barrier = pltpu.get_barrier_semaphore()
@@ -109,7 +110,7 @@
     def place(k):
         step = lax.div(k + 1, 2)
         away = jnp.where(lax.rem(k, 2) == 1, 4 - step, 4 + step)
-        return lax.rem(high + lax.rem(away, 8), 8)
+        return lax.rem(high + jnp.where(mirrored, 8 - away, away), 8)
 
     def xcopy(k):
         start = pl.multiple_of(place(k) * BRICK, BRICK)
@@ -252,7 +253,7 @@
         slot(k, 1, second=first, last=last, last_brick=last, late=late)
 
     def send(k, j):
-        chunk = lax.rem(low + AWAY[j], 8)
+        chunk = lax.rem(low + jnp.where(mirrored, 8 - AWAY[j], AWAY[j]), 8)
         owner = place(k) * 8 + chunk
         way, target = 0, owner
         if RING[AWAY[j]] >= 2:

time: 30.5 us -> 30.4 us (level)
  no operation moved by 1% of the time
where the time goes in v6:
time: 30.4 us; the launch traced here: 30.1 us
  Pallas kernels  28.9 us (95%)
  between operations  0.66 us (2%)
  local copies, waits for them, and re-layouts  0.58 us (2%)
    pallas_call x1, Pallas kernels, per_device(): pl.pallas_call(functools.partial(kernel, slabs=slabs), out_shape=jax.Shap...  28.9 us

profile of v6, /device:TPU:1, one launch (start us, length us, event | category | flops | bytes accessed | tf_op | source)
XLA Modules:
  0.0 30.1 jit_solution(13289371494877770087)
XLA Ops:
  0.7 28.9 %shard_map.91 = f32[4,128]{1,0:T(4,128)S(1)} custom-call(bf16[32,4,8192]{2,1,0:T(4,128)(2,1)} %refs_0_.1, s32[2,64,128]{2,1,0:T(8,128)} %bitcast.5, s32[1]{0:T(128)S(6)} %copy.11.refs_2_, bf16[32,128]{1,0:T(8,128)(2,1)} %bitcast.6, bf16[128,128]{1,0:T(8,128)(2,1)} %refs_4_.1, bf16[4,128]{1,0:T(4,128)(2,1)} %refs_5_.1, f32[1,128]{1,0:T(1,128)} %bitcast.7, ...), custom_call_target="tpu_custom_call" | custom-call | tf_op jit(solution)/shard_map/pallas_call | solution.py:391
  29.6 0.6 %copy.12 = f32[4,128]{1,0:T(4,128)} copy(f32[4,128]{1,0:T(4,128)S(1)} %shard_map.91) | data formatting | bytes 4096

commit v7 on v6

--- a/solution.py
+++ b/solution.py
@@ -88,25 +88,6 @@
     mirrored = lax.rem(lax.axis_index("tile"), 2) == 1
     spacing = 6.0 / (4 * slabs)
 
-    barrier = pltpu.get_barrier_semaphore()
-
-    def greet(dx, dz):
-        peer = lax.rem(high + dx, 8) * 8 + lax.rem(low + dz, 8)
-        pl.semaphore_signal(barrier, inc=1, device_id={"depth": peer}, device_id_type=MESH)
-
-    @pl.when(low < 6)
-    def _():
-        for dx, dz in FAR:
-            greet(dx, dz)
-
-    for dx, dz in PEERS:
-        if (dx, dz) not in FAR:
-            greet(dx, dz)
-
-    by_relay = jnp.where(
-        (low == 2) | (low == 3), 8, jnp.where((low == 1) | (low == 4), 4, jnp.where((low == 0) | (low == 5), 1, 0))
-    )
-
     def place(k):
         step = lax.div(k + 1, 2)
         away = jnp.where(lax.rem(k, 2) == 1, 4 - step, 4 + step)
@@ -132,6 +113,26 @@
         copy.start()
     for k in range(1, bricks):
         xcopy(k).start()
+
+    barrier = pltpu.get_barrier_semaphore()
+
+    def greet(dx, dz):
+        peer = lax.rem(high + dx, 8) * 8 + lax.rem(low + dz, 8)
+        pl.semaphore_signal(barrier, inc=1, device_id={"depth": peer}, device_id_type=MESH)
+
+    @pl.when(low < 6)
+    def _():
+        for dx, dz in FAR:
+            greet(dx, dz)
+
+    for dx, dz in PEERS:
+        if (dx, dz) not in FAR:
+            greet(dx, dz)
+
+    by_relay = jnp.where(
+        (low == 2) | (low == 3), 8, jnp.where((low == 1) | (low == 4), 4, jnp.where((low == 0) | (low == 5), 1, 0))
+    )
+
     for copy in small:
         copy.wait()
 

time: 30.4 us -> 30.5 us (level); the launches traced: 30.1 us -> 29.9 us
  no operation moved by 1% of the time
where the time goes in v7:
time: 30.5 us; the launch traced here: 29.9 us
  Pallas kernels  28.6 us (94%)
  between operations  0.66 us (2%)
  local copies, waits for them, and re-layouts  0.58 us (2%)
    pallas_call x1, Pallas kernels, per_device(): pl.pallas_call(functools.partial(kernel, slabs=slabs), out_shape=jax.Shap...  28.6 us

profile of v7, /device:TPU:1, one launch (start us, length us, event | category | flops | bytes accessed | tf_op | source)
XLA Modules:
  0.0 29.9 jit_solution(1417686655423110330)
XLA Ops:
  0.7 28.6 %shard_map.91 = f32[4,128]{1,0:T(4,128)S(1)} custom-call(bf16[32,4,8192]{2,1,0:T(4,128)(2,1)} %refs_0_.1, s32[2,64,128]{2,1,0:T(8,128)} %bitcast.5, s32[1]{0:T(128)S(6)} %copy.11.refs_2_, bf16[32,128]{1,0:T(8,128)(2,1)} %bitcast.6, bf16[128,128]{1,0:T(8,128)(2,1)} %refs_4_.1, bf16[4,128]{1,0:T(4,128)(2,1)} %refs_5_.1, f32[1,128]{1,0:T(1,128)} %bitcast.7, ...), custom_call_target="tpu_custom_call" | custom-call | tf_op jit(solution)/shard_map/pallas_call | solution.py:392
  29.3 0.6 %copy.12 = f32[4,128]{1,0:T(4,128)} copy(f32[4,128]{1,0:T(4,128)S(1)} %shard_map.91) | data formatting | bytes 4096

commit v8 on v7

--- a/solution.py
+++ b/solution.py
@@ -316,13 +316,12 @@
     def step(k, _):
         brick(k, late=lambda: finish(k - 1))
 
-        @pl.when(k == 3)
+        @pl.when(k == 2)
         def _():
             pl.semaphore_wait(barrier, slabs - 1 - by_relay)
             send_brick(0)
-            send_brick(1)
-
-        @pl.when(k >= 3)
+
+        @pl.when(k >= 2)
         def _():
             send_brick(k - 1)
 

time: 30.5 us -> 30.8 us (level)
  the two profiles are of different devices: /device:TPU:1 before, /device:TPU:96 now
where the time goes in v8:
time: 30.8 us; the launch traced here: 30.7 us
  Pallas kernels  29.4 us (95%)
  between operations  0.66 us (2%)
  local copies, waits for them, and re-layouts  0.58 us (2%)
    pallas_call x1, Pallas kernels, per_device(): pl.pallas_call(functools.partial(kernel, slabs=slabs), out_shape=jax.Shap...  29.4 us

profile of v8, /device:TPU:96, one launch (start us, length us, event | category | flops | bytes accessed | tf_op | source)
XLA Modules:
  0.0 30.7 jit_solution(6044113137545572601)
XLA Ops:
  0.7 29.4 %shard_map.91 = f32[4,128]{1,0:T(4,128)S(1)} custom-call(bf16[32,4,8192]{2,1,0:T(4,128)(2,1)} %refs_0_.1, s32[2,64,128]{2,1,0:T(8,128)} %bitcast.5, s32[1]{0:T(128)S(6)} %copy.11.refs_2_, bf16[32,128]{1,0:T(8,128)(2,1)} %bitcast.6, bf16[128,128]{1,0:T(8,128)(2,1)} %refs_4_.1, bf16[4,128]{1,0:T(4,128)(2,1)} %refs_5_.1, f32[1,128]{1,0:T(1,128)} %bitcast.7, ...), custom_call_target="tpu_custom_call" | custom-call | tf_op jit(solution)/shard_map/pallas_call | solution.py:391
  30.1 0.6 %copy.12 = f32[4,128]{1,0:T(4,128)} copy(f32[4,128]{1,0:T(4,128)S(1)} %shard_map.91) | data formatting | bytes 4096

commit v9 on v7

--- a/solution.py
+++ b/solution.py
@@ -316,13 +316,14 @@
     def step(k, _):
         brick(k, late=lambda: finish(k - 1))
 
-        @pl.when(k == 3)
+        @pl.when(k == 4)
         def _():
             pl.semaphore_wait(barrier, slabs - 1 - by_relay)
             send_brick(0)
             send_brick(1)
-
-        @pl.when(k >= 3)
+            send_brick(2)
+
+        @pl.when(k >= 4)
         def _():
             send_brick(k - 1)
 

time: 30.5 us -> 30.4 us (level); the launches traced: 29.9 us -> 30.2 us
  Pallas kernels: 28.6 us -> 29 us
    pallas_call x1, Pallas kernels: 28.6 us -> 29 us  [per_device(): pl.pallas_call(functools.partial(kernel, slabs=slabs), out_shape=jax.Shap...]
where the time goes in v9:
time: 30.4 us; the launch traced here: 30.2 us
  Pallas kernels  29 us (95%)
  between operations  0.66 us (2%)
  local copies, waits for them, and re-layouts  0.58 us (2%)
    pallas_call x1, Pallas kernels, per_device(): pl.pallas_call(functools.partial(kernel, slabs=slabs), out_shape=jax.Shap...  29 us

profile of v9, /device:TPU:1, one launch (start us, length us, event | category | flops | bytes accessed | tf_op | source)
XLA Modules:
  0.0 30.2 jit_solution(5913121181131776831)
XLA Ops:
  0.7 29.0 %shard_map.91 = f32[4,128]{1,0:T(4,128)S(1)} custom-call(bf16[32,4,8192]{2,1,0:T(4,128)(2,1)} %refs_0_.1, s32[2,64,128]{2,1,0:T(8,128)} %bitcast.5, s32[1]{0:T(128)S(6)} %copy.11.refs_2_, bf16[32,128]{1,0:T(8,128)(2,1)} %bitcast.6, bf16[128,128]{1,0:T(8,128)(2,1)} %refs_4_.1, bf16[4,128]{1,0:T(4,128)(2,1)} %refs_5_.1, f32[1,128]{1,0:T(1,128)} %bitcast.7, ...), custom_call_target="tpu_custom_call" | custom-call | tf_op jit(solution)/shard_map/pallas_call | solution.py:393
  29.6 0.6 %copy.12 = f32[4,128]{1,0:T(4,128)} copy(f32[4,128]{1,0:T(4,128)S(1)} %shard_map.91) | data formatting | bytes 4096
